TPU v7x, 256 devices: a whole 4x4x8 slice. The times are simulated.
256 devices in a mesh: grp: 16 (over y, x_hi, core), dom: 16 (over z, x_lo).
Axes of the slice: x: 4 (x_hi: 2, x_lo: 2; x = x_hi * 2 + x_lo), y: 4, z: 8, core: 2. Of those that a mesh axis runs over, the one named last changes fastest.
Arguments:
- queries: bfloat16 [65536, 256], P(('grp', 'dom')), may hold values from -6 to 6
- key_rows: bfloat16 [65536, 256], P(('grp', 'dom')), may hold values from -6 to 6
- value_rows: bfloat16 [65536, 256], P(('grp', 'dom')), may hold values from -6 to 6
- saved_output: bfloat16 [65536, 256], P(('grp', 'dom')), may hold values from -6 to 6
- output_grad: bfloat16 [65536, 256], P(('grp', 'dom')), may hold values from -24 to 24
- log_norm: float32 [8, 65536], P(None, ('grp', 'dom')), may hold values from 5 to 8
- local_lists: int32 [512, 32], P(('grp', 'dom')), may hold values from 0 to 31, as said below
- expander_lists: int32 [512, 16], P(('grp', 'dom')), may hold values from 0 to 31, as said below
- local_counts: int32 [512], P(('grp', 'dom')), may hold values from 1 to 32, as said below
- expander_counts: int32 [512], P(('grp', 'dom')), may hold values from 1 to 16, as said below
Outputs:
- query_grad: bfloat16 [65536, 256], P(('grp', 'dom'))
- key_grad: bfloat16 [65536, 256], P(('grp', 'dom'))
- value_grad: bfloat16 [65536, 256], P(('grp', 'dom'))
Inputs may be any that keep to these rules, and one draw needn't show every extreme that they name: `local_lists`: each row is an ordering of all 32 blocks of the partition. `expander_lists`: entries of a row are distinct and never name the block's own partition. `local_counts`: some block uses its whole list. `expander_counts`: some block uses its whole list.
All inputs are finite; a program needn't handle non-finite values.
Results may differ from a plain program's by a relative error of at most 0.0054.
Values may be sent and summed in bfloat16 or wider, within the bound.
A program may use at most 128 MiB of HBM per device.

v0:
```python
import math

import jax
import jax.numpy as jnp
from jax import lax
from jax.sharding import PartitionSpec as P

HEADS = 8
HEAD_DIM = 32
BLOCK = 128


def shifted(value, axis, steps):
    count = lax.axis_size(axis)
    pairs = [(source, (source + steps) % count) for source in range(count)]
    return lax.ppermute(value, axis, pairs)


def attention_parts(query_side, near_keys, near_values, visible):
    query_blocks, grad_blocks, lse3, delta3 = query_side
    scaling = 1.0 / math.sqrt(HEAD_DIM)
    scores = jnp.einsum(
        "bqhd,ckhd->bchqk", query_blocks, near_keys, preferred_element_type=jnp.float32
    )
    attention = (
        jnp.exp(scaling * scores - lse3[:, None, :, :, None]) * visible[:, :, None, None, None]
    )
    grad_p = jnp.einsum(
        "bqhd,ckhd->bchqk", grad_blocks, near_values, preferred_element_type=jnp.float32
    )
    score_grad = (attention * (grad_p - delta3[:, None, :, :, None])).astype(jnp.bfloat16)
    return (attention, score_grad)


def split_visiting(visiting):
    holding = visiting.shape[1] // BLOCK
    near_keys = visiting[0].reshape(holding, BLOCK, HEADS, HEAD_DIM)
    near_values = visiting[1].reshape(holding, BLOCK, HEADS, HEAD_DIM)
    return (holding, near_keys, near_values)


def key_side_terms(query_side, attention, score_grad, holding):
    scaling = 1.0 / math.sqrt(HEAD_DIM)
    query_blocks, grad_blocks = (query_side[0], query_side[1])
    attention_low = attention.astype(jnp.bfloat16)
    grad_v = jnp.einsum(
        "bchqk,bqhd->ckhd", attention_low, grad_blocks, preferred_element_type=jnp.float32
    )
    grad_k = scaling * jnp.einsum(
        "bchqk,bqhd->ckhd", score_grad, query_blocks, preferred_element_type=jnp.float32
    )
    width = HEADS * HEAD_DIM
    return jnp.stack(
        [grad_k.reshape(holding * BLOCK, width), grad_v.reshape(holding * BLOCK, width)]
    )


def pair_terms(query_side, visiting, visible):
    holding, near_keys, near_values = split_visiting(visiting)
    attention, score_grad = attention_parts(query_side, near_keys, near_values, visible)
    scaling = 1.0 / math.sqrt(HEAD_DIM)
    grad_q = scaling * jnp.einsum(
        "bchqk,ckhd->bqhd", score_grad, near_keys, preferred_element_type=jnp.float32
    )
    partial_value = key_side_terms(query_side, attention, score_grad, holding)
    return (grad_q, partial_value)


def block_hits(lists, counts, anchor, holding):
    slots = lists.shape[1]
    live = jnp.arange(slots, dtype=jnp.int32)[None, :] < counts[:, None]
    targets = anchor * holding + jnp.arange(holding, dtype=jnp.int32)
    matched = (lists[:, :, None] == targets[None, None, :]) & live[:, :, None]
    return jnp.any(matched, axis=1).astype(jnp.float32)


def contribution(query_side, lists, counts, anchor, visiting):
    holding = lists.shape[0]
    visible = block_hits(lists, counts, anchor, holding)
    nothing_q = jnp.zeros(query_side[0].shape, jnp.float32)
    nothing_part = jnp.zeros(visiting.shape, jnp.float32)
    return lax.cond(
        jnp.any(visible > 0.0),
        lambda: pair_terms(query_side, visiting, visible),
        lambda: (nothing_q, nothing_part),
    )


def circulate(length, position, lists, counts, query_side, key_block, send_keys, send_grads):

    def advance(turn, carry):
        visiting, partial_value, grad_q = carry
        anchor = (position - turn) % length
        add_q, add_part = contribution(query_side, lists, counts, anchor, visiting)
        return (send_keys(visiting), send_grads(partial_value + add_part), grad_q + add_q)

    start = (
        key_block,
        jnp.zeros(key_block.shape, jnp.float32),
        jnp.zeros(query_side[0].shape, jnp.float32),
    )
    visiting, partial_value, grad_q = lax.fori_loop(0, length - 1, advance, start)
    add_q, add_part = contribution(
        query_side, lists, counts, (position - length + 1) % length, visiting
    )
    return (grad_q + add_q, send_grads(partial_value + add_part))


def body(
    queries,
    key_rows,
    value_rows,
    saved_output,
    output_grad,
    log_norm,
    local_lists,
    expander_lists,
    local_counts,
    expander_counts,
):
    holding = local_lists.shape[0]
    shape4 = (holding, BLOCK, HEADS, HEAD_DIM)
    query_blocks = queries.reshape(shape4)
    grad_blocks = output_grad.reshape(shape4)
    products = output_grad.astype(jnp.float32) * saved_output.astype(jnp.float32)
    delta_rows = jnp.sum(products.reshape(holding * BLOCK, HEADS, HEAD_DIM), axis=2)
    delta3 = delta_rows.reshape(holding, BLOCK, HEADS).transpose(0, 2, 1)
    lse3 = log_norm.reshape(HEADS, holding, BLOCK).transpose(1, 0, 2)
    query_side = (query_blocks, grad_blocks, lse3, delta3)
    key_block = jnp.stack([key_rows, value_rows])
    groups = lax.axis_size("grp")
    domains = lax.axis_size("dom")
    grad_local, part_local = circulate(
        groups,
        lax.axis_index("grp"),
        local_lists,
        local_counts,
        query_side,
        key_block,
        lambda block: shifted(block, "grp", 1),
        lambda partial_value: shifted(partial_value, "grp", 1),
    )
    grad_far, part_far = circulate(
        domains,
        lax.axis_index("dom"),
        expander_lists,
        expander_counts,
        query_side,
        key_block,
        lambda block: shifted(block, "dom", 1),
        lambda partial_value: shifted(partial_value, "dom", 1),
    )
    query_grad = (
        (grad_local + grad_far).reshape(holding * BLOCK, HEADS * HEAD_DIM).astype(jnp.bfloat16)
    )
    combined = part_local + part_far
    return (query_grad, combined[0].astype(jnp.bfloat16), combined[1].astype(jnp.bfloat16))


def solution(mesh):
    placed = (
        P(("grp", "dom"), None),
        P(("grp", "dom"), None),
        P(("grp", "dom"), None),
        P(("grp", "dom"), None),
        P(("grp", "dom"), None),
        P(None, ("grp", "dom")),
        P(("grp", "dom"), None),
        P(("grp", "dom"), None),
        P(("grp", "dom")),
        P(("grp", "dom")),
    )
    return jax.shard_map(
        body,
        mesh=mesh,
        in_specs=placed,
        out_specs=(P(("grp", "dom"), None), P(("grp", "dom"), None), P(("grp", "dom"), None)),
        check_vma=False,
    )
```

profile of v0, /device:TPU:160, one launch (start us, length us, event | category | flops | bytes accessed | tf_op | source)
XLA Modules:
  0.0 1021.6 jit_solution(4081725707218284849)
XLA Ops:
  11.1 492.4 %while.41 = (s32[]{:T(128)}, bf16[2,256,256]{1,2,0:T(8,128)(2,1)}, f32[2,256,256]{1,2,0:T(8,128)}, f32[2,128,8,32]{1,3,0,2:T(8,128)}, s32[2,16]{1,0:T(2,128)S(1)...) while((s32[]{:T(128)}, bf16[2,256,256]{1,2,0:T(8,128)(2,1)}, ...), condition=%wide.region_16.17_spmd.clone, body=%wide.region_11.16_spmd.clone.sunk | while | flops 171966720 | bytes 23479648 | solution.py:102
  21.5 16.1 %collective-permute-done.2 = bf16[2,256,256]{1,2,0:T(8,128)(2,1)} collective-permute-done((bf16[2,256,256]{1,2,0:T(8,128)(2,1)}, bf16[2,256,256]{1,2,0:T(8,128)(2,1)}, u32[]{:S(2)}, u32[]{:S(2)}) %collective-permute-start.2) | collective-permute-done | bytes 262176 | tf_op jit(solution)/shard_map/while/body/eval_jaxpr/ppermute | solution.py:16
  55.5 17.5 %collective-permute-done.2 = bf16[2,256,256]{1,2,0:T(8,128)(2,1)} collective-permute-done((bf16[2,256,256]{1,2,0:T(8,128)(2,1)}, bf16[2,256,256]{1,2,0:T(8,128)(2,1)}, u32[]{:S(2)}, u32[]{:S(2)}) %collective-permute-start.2) | collective-permute-done | bytes 262176 | tf_op jit(solution)/shard_map/while/body/eval_jaxpr/ppermute | solution.py:16
  90.7 15.6 %collective-permute-done.2 = bf16[2,256,256]{1,2,0:T(8,128)(2,1)} collective-permute-done((bf16[2,256,256]{1,2,0:T(8,128)(2,1)}, bf16[2,256,256]{1,2,0:T(8,128)(2,1)}, u32[]{:S(2)}, u32[]{:S(2)}) %collective-permute-start.2) | collective-permute-done | bytes 262176 | tf_op jit(solution)/shard_map/while/body/eval_jaxpr/ppermute | solution.py:16
  125.1 10.9 %collective-permute-done.2 = bf16[2,256,256]{1,2,0:T(8,128)(2,1)} collective-permute-done((bf16[2,256,256]{1,2,0:T(8,128)(2,1)}, bf16[2,256,256]{1,2,0:T(8,128)(2,1)}, u32[]{:S(2)}, u32[]{:S(2)}) %collective-permute-start.2) | collective-permute-done | bytes 262176 | tf_op jit(solution)/shard_map/while/body/eval_jaxpr/ppermute | solution.py:16
  144.4 12.5 %collective-permute-start.2 = (bf16[2,256,256]{1,2,0:T(8,128)(2,1)}, bf16[2,256,256]{1,2,0:T(8,128)(2,1)}, u32[]{:S(2)}, u32[]{:S(2)}) collective-permute-start(bf16[2,256,256]{1,2,0:T(8,128)(2,1)} %copy.282), channel_id=1, source_target_pairs={{0,1},{1,2},{2,3},{3,4},{4,5},{5,6},{6,7},{7,8},{8,9},{9,10},{10,1... | collective-permute-start | bytes 786440 | tf_op jit(solution)/shard_map/while/body/eval_jaxpr/ppermute | solution.py:16
  181.7 12.4 %collective-permute-start.2 = (bf16[2,256,256]{1,2,0:T(8,128)(2,1)}, bf16[2,256,256]{1,2,0:T(8,128)(2,1)}, u32[]{:S(2)}, u32[]{:S(2)}) collective-permute-start(bf16[2,256,256]{1,2,0:T(8,128)(2,1)} %copy.282), channel_id=1, source_target_pairs={{0,1},{1,2},{2,3},{3,4},{4,5},{5,6},{6,7},{7,8},{8,9},{9,10},{10,1... | collective-permute-start | bytes 786440 | tf_op jit(solution)/shard_map/while/body/eval_jaxpr/ppermute | solution.py:16
  235.8 18.2 %collective-permute-start.3 = (f32[2,256,256]{1,2,0:T(8,128)S(1)}, f32[2,256,256]{1,2,0:T(8,128)S(1)}, u32[]{:S(2)}, u32[]{:S(2)}) collective-permute-start(f32[2,256,256]{1,2,0:T(8,128)S(1)} %add.258), channel_id=1, source_target_pairs={{0,1},{1,2},{2,3},{3,4},{4,5},{5,6},{6,7},{7,8},{8,9},{9,10},{10,1... | collective-permute-start | bytes 1572872 | tf_op jit(solution)/shard_map/while/body/eval_jaxpr/ppermute | solution.py:16
  293.0 11.6 %collective-permute-done.2 = bf16[2,256,256]{1,2,0:T(8,128)(2,1)} collective-permute-done((bf16[2,256,256]{1,2,0:T(8,128)(2,1)}, bf16[2,256,256]{1,2,0:T(8,128)(2,1)}, u32[]{:S(2)}, u32[]{:S(2)}) %collective-permute-start.2) | collective-permute-done | bytes 262176 | tf_op jit(solution)/shard_map/while/body/eval_jaxpr/ppermute | solution.py:16
  322.5 15.1 %collective-permute-done.2 = bf16[2,256,256]{1,2,0:T(8,128)(2,1)} collective-permute-done((bf16[2,256,256]{1,2,0:T(8,128)(2,1)}, bf16[2,256,256]{1,2,0:T(8,128)(2,1)}, u32[]{:S(2)}, u32[]{:S(2)}) %collective-permute-start.2) | collective-permute-done | bytes 262176 | tf_op jit(solution)/shard_map/while/body/eval_jaxpr/ppermute | solution.py:16
  358.0 16.1 %collective-permute-done.2 = bf16[2,256,256]{1,2,0:T(8,128)(2,1)} collective-permute-done((bf16[2,256,256]{1,2,0:T(8,128)(2,1)}, bf16[2,256,256]{1,2,0:T(8,128)(2,1)}, u32[]{:S(2)}, u32[]{:S(2)}) %collective-permute-start.2) | collective-permute-done | bytes 262176 | tf_op jit(solution)/shard_map/while/body/eval_jaxpr/ppermute | solution.py:16
  381.0 11.6 %collective-permute-start.3 = (f32[2,256,256]{1,2,0:T(8,128)S(1)}, f32[2,256,256]{1,2,0:T(8,128)S(1)}, u32[]{:S(2)}, u32[]{:S(2)}) collective-permute-start(f32[2,256,256]{1,2,0:T(8,128)S(1)} %add.258), channel_id=1, source_target_pairs={{0,1},{1,2},{2,3},{3,4},{4,5},{5,6},{6,7},{7,8},{8,9},{9,10},{10,1... | collective-permute-start | bytes 1572872 | tf_op jit(solution)/shard_map/while/body/eval_jaxpr/ppermute | solution.py:16
  395.2 14.5 %collective-permute-done.2 = bf16[2,256,256]{1,2,0:T(8,128)(2,1)} collective-permute-done((bf16[2,256,256]{1,2,0:T(8,128)(2,1)}, bf16[2,256,256]{1,2,0:T(8,128)(2,1)}, u32[]{:S(2)}, u32[]{:S(2)}) %collective-permute-start.2) | collective-permute-done | bytes 262176 | tf_op jit(solution)/shard_map/while/body/eval_jaxpr/ppermute | solution.py:16
  416.6 11.6 %collective-permute-start.3 = (f32[2,256,256]{1,2,0:T(8,128)S(1)}, f32[2,256,256]{1,2,0:T(8,128)S(1)}, u32[]{:S(2)}, u32[]{:S(2)}) collective-permute-start(f32[2,256,256]{1,2,0:T(8,128)S(1)} %add.258), channel_id=1, source_target_pairs={{0,1},{1,2},{2,3},{3,4},{4,5},{5,6},{6,7},{7,8},{8,9},{9,10},{10,1... | collective-permute-start | bytes 1572872 | tf_op jit(solution)/shard_map/while/body/eval_jaxpr/ppermute | solution.py:16
  477.5 12.7 %collective-permute-start.3 = (f32[2,256,256]{1,2,0:T(8,128)S(1)}, f32[2,256,256]{1,2,0:T(8,128)S(1)}, u32[]{:S(2)}, u32[]{:S(2)}) collective-permute-start(f32[2,256,256]{1,2,0:T(8,128)S(1)} %add.258), channel_id=1, source_target_pairs={{0,1},{1,2},{2,3},{3,4},{4,5},{5,6},{6,7},{7,8},{8,9},{9,10},{10,1... | collective-permute-start | bytes 1572872 | tf_op jit(solution)/shard_map/while/body/eval_jaxpr/ppermute | solution.py:16
  509.2 21.9 %collective-permute-start.5 = (f32[2,256,256]{2,1,0:T(8,128)}, f32[2,256,256]{2,1,0:T(8,128)}, u32[]{:S(2)}, u32[]{:S(2)}) collective-permute-start(f32[2,256,256]{2,1,0:T(8,128)} %add.207), channel_id=1, source_target_pairs={{0,1},{1,2},{2,3},{3,4},{4,5},{5,6},{6,7},{7,8},{8,9},{9,10},{10,1... | collective-permute-start | bytes 1572872 | tf_op jit(solution)/shard_map/ppermute | solution.py:16
  535.4 455.4 %while.40 = (s32[]{:T(128)}, bf16[2,256,256]{1,2,0:T(8,128)(2,1)}, f32[2,256,256]{1,2,0:T(8,128)}, f32[2,128,8,32]{1,3,0,2:T(8,128)}, s32[2,32]{1,0:T(2,128)S(1)...) while((s32[]{:T(128)}, bf16[2,256,256]{1,2,0:T(8,128)(2,1)}, ...), condition=%wide.region_6.7_spmd.clone, body=%wide.region_1.6_spmd.clone.sunk | while | flops 171966944 | bytes 23480352 | solution.py:102
  577.0 13.2 %collective-permute-done = bf16[2,256,256]{1,2,0:T(8,128)(2,1)} collective-permute-done((bf16[2,256,256]{1,2,0:T(8,128)(2,1)}, bf16[2,256,256]{1,2,0:T(8,128)(2,1)}, u32[]{:S(2)}, u32[]{:S(2)}) %collective-permute-start) | collective-permute-done | bytes 262176 | tf_op jit(solution)/shard_map/while/body/eval_jaxpr/ppermute | solution.py:16
  608.2 13.2 %collective-permute-done = bf16[2,256,256]{1,2,0:T(8,128)(2,1)} collective-permute-done((bf16[2,256,256]{1,2,0:T(8,128)(2,1)}, bf16[2,256,256]{1,2,0:T(8,128)(2,1)}, u32[]{:S(2)}, u32[]{:S(2)}) %collective-permute-start) | collective-permute-done | bytes 262176 | tf_op jit(solution)/shard_map/while/body/eval_jaxpr/ppermute | solution.py:16
  639.5 13.2 %collective-permute-done = bf16[2,256,256]{1,2,0:T(8,128)(2,1)} collective-permute-done((bf16[2,256,256]{1,2,0:T(8,128)(2,1)}, bf16[2,256,256]{1,2,0:T(8,128)(2,1)}, u32[]{:S(2)}, u32[]{:S(2)}) %collective-permute-start) | collective-permute-done | bytes 262176 | tf_op jit(solution)/shard_map/while/body/eval_jaxpr/ppermute | solution.py:16
  670.7 13.2 %collective-permute-done = bf16[2,256,256]{1,2,0:T(8,128)(2,1)} collective-permute-done((bf16[2,256,256]{1,2,0:T(8,128)(2,1)}, bf16[2,256,256]{1,2,0:T(8,128)(2,1)}, u32[]{:S(2)}, u32[]{:S(2)}) %collective-permute-start) | collective-permute-done | bytes 262176 | tf_op jit(solution)/shard_map/while/body/eval_jaxpr/ppermute | solution.py:16
  701.9 13.2 %collective-permute-done = bf16[2,256,256]{1,2,0:T(8,128)(2,1)} collective-permute-done((bf16[2,256,256]{1,2,0:T(8,128)(2,1)}, bf16[2,256,256]{1,2,0:T(8,128)(2,1)}, u32[]{:S(2)}, u32[]{:S(2)}) %collective-permute-start) | collective-permute-done | bytes 262176 | tf_op jit(solution)/shard_map/while/body/eval_jaxpr/ppermute | solution.py:16
  733.1 13.2 %collective-permute-done = bf16[2,256,256]{1,2,0:T(8,128)(2,1)} collective-permute-done((bf16[2,256,256]{1,2,0:T(8,128)(2,1)}, bf16[2,256,256]{1,2,0:T(8,128)(2,1)}, u32[]{:S(2)}, u32[]{:S(2)}) %collective-permute-start) | collective-permute-done | bytes 262176 | tf_op jit(solution)/shard_map/while/body/eval_jaxpr/ppermute | solution.py:16
  764.3 13.2 %collective-permute-done = bf16[2,256,256]{1,2,0:T(8,128)(2,1)} collective-permute-done((bf16[2,256,256]{1,2,0:T(8,128)(2,1)}, bf16[2,256,256]{1,2,0:T(8,128)(2,1)}, u32[]{:S(2)}, u32[]{:S(2)}) %collective-permute-start) | collective-permute-done | bytes 262176 | tf_op jit(solution)/shard_map/while/body/eval_jaxpr/ppermute | solution.py:16
  795.5 13.2 %collective-permute-done = bf16[2,256,256]{1,2,0:T(8,128)(2,1)} collective-permute-done((bf16[2,256,256]{1,2,0:T(8,128)(2,1)}, bf16[2,256,256]{1,2,0:T(8,128)(2,1)}, u32[]{:S(2)}, u32[]{:S(2)}) %collective-permute-start) | collective-permute-done | bytes 262176 | tf_op jit(solution)/shard_map/while/body/eval_jaxpr/ppermute | solution.py:16
  826.8 13.2 %collective-permute-done = bf16[2,256,256]{1,2,0:T(8,128)(2,1)} collective-permute-done((bf16[2,256,256]{1,2,0:T(8,128)(2,1)}, bf16[2,256,256]{1,2,0:T(8,128)(2,1)}, u32[]{:S(2)}, u32[]{:S(2)}) %collective-permute-start) | collective-permute-done | bytes 262176 | tf_op jit(solution)/shard_map/while/body/eval_jaxpr/ppermute | solution.py:16
  848.9 16.2 %collective-permute-done = bf16[2,256,256]{1,2,0:T(8,128)(2,1)} collective-permute-done((bf16[2,256,256]{1,2,0:T(8,128)(2,1)}, bf16[2,256,256]{1,2,0:T(8,128)(2,1)}, u32[]{:S(2)}, u32[]{:S(2)}) %collective-permute-start) | collective-permute-done | bytes 262176 | tf_op jit(solution)/shard_map/while/body/eval_jaxpr/ppermute | solution.py:16
  883.1 13.2 %collective-permute-done = bf16[2,256,256]{1,2,0:T(8,128)(2,1)} collective-permute-done((bf16[2,256,256]{1,2,0:T(8,128)(2,1)}, bf16[2,256,256]{1,2,0:T(8,128)(2,1)}, u32[]{:S(2)}, u32[]{:S(2)}) %collective-permute-start) | collective-permute-done | bytes 262176 | tf_op jit(solution)/shard_map/while/body/eval_jaxpr/ppermute | solution.py:16
  914.3 13.2 %collective-permute-done = bf16[2,256,256]{1,2,0:T(8,128)(2,1)} collective-permute-done((bf16[2,256,256]{1,2,0:T(8,128)(2,1)}, bf16[2,256,256]{1,2,0:T(8,128)(2,1)}, u32[]{:S(2)}, u32[]{:S(2)}) %collective-permute-start) | collective-permute-done | bytes 262176 | tf_op jit(solution)/shard_map/while/body/eval_jaxpr/ppermute | solution.py:16
  945.5 13.2 %collective-permute-done = bf16[2,256,256]{1,2,0:T(8,128)(2,1)} collective-permute-done((bf16[2,256,256]{1,2,0:T(8,128)(2,1)}, bf16[2,256,256]{1,2,0:T(8,128)(2,1)}, u32[]{:S(2)}, u32[]{:S(2)}) %collective-permute-start) | collective-permute-done | bytes 262176 | tf_op jit(solution)/shard_map/while/body/eval_jaxpr/ppermute | solution.py:16
  976.8 13.2 %collective-permute-done = bf16[2,256,256]{1,2,0:T(8,128)(2,1)} collective-permute-done((bf16[2,256,256]{1,2,0:T(8,128)(2,1)}, bf16[2,256,256]{1,2,0:T(8,128)(2,1)}, u32[]{:S(2)}, u32[]{:S(2)}) %collective-permute-start) | collective-permute-done | bytes 262176 | tf_op jit(solution)/shard_map/while/body/eval_jaxpr/ppermute | solution.py:16
  992.8 13.4 %conditional.4 = (f32[2,128,8,32]{1,3,0,2:T(8,128)}, f32[2,256,256]{2,1,0:T(8,128)}) conditional(s32[]{:T(128)} %convert_element_type.99, () %tuple.85, (bf16[2,256,256]{1,2,0:T(8,128)(2,1)}, bf16[2,128,8,32]{1,0,3,2:T(2,128)(2,1)}, f32[2,8,128]{2,0,1:T(2,128)S(1)}, f32[2,2]{1,0:T(2,128)}, bf16[2,128,8,32]{1,0,3,2:T(2,128)(2,1)}, ...), branch_computations={%region_9.10_spmd, %region_10.11_spmd} | conditional | flops 171704320 | bytes 17973396 | solution.py:82
  (883 shorter events, 812.4 us)
Async XLA Ops:
  17.2 20.4 %collective-permute-start.3 = (f32[2,256,256]{1,2,0:T(8,128)S(1)}, f32[2,256,256]{1,2,0:T(8,128)S(1)}, u32[]{:S(2)}, u32[]{:S(2)}) collective-permute-start(f32[2,256,256]{1,2,0:T(8,128)S(1)} %add.258), channel_id=1, source_target_pairs={{0,1},{1,2},{2,3},{3,4},{4,5},{5,6},{6,7},{7,8},{8,9},{9,10},{10,1... | collective-permute-start | bytes 1572872 | tf_op jit(solution)/shard_map/while/body/eval_jaxpr/ppermute | solution.py:16
  18.8 18.8 %collective-permute-start.2 = (bf16[2,256,256]{1,2,0:T(8,128)(2,1)}, bf16[2,256,256]{1,2,0:T(8,128)(2,1)}, u32[]{:S(2)}, u32[]{:S(2)}) collective-permute-start(bf16[2,256,256]{1,2,0:T(8,128)(2,1)} %copy.282), channel_id=1, source_target_pairs={{0,1},{1,2},{2,3},{3,4},{4,5},{5,6},{6,7},{7,8},{8,9},{9,10},{10,1... | collective-permute-start | bytes 786440 | tf_op jit(solution)/shard_map/while/body/eval_jaxpr/ppermute | solution.py:16
  53.6 19.5 %collective-permute-start.3 = (f32[2,256,256]{1,2,0:T(8,128)S(1)}, f32[2,256,256]{1,2,0:T(8,128)S(1)}, u32[]{:S(2)}, u32[]{:S(2)}) collective-permute-start(f32[2,256,256]{1,2,0:T(8,128)S(1)} %add.258), channel_id=1, source_target_pairs={{0,1},{1,2},{2,3},{3,4},{4,5},{5,6},{6,7},{7,8},{8,9},{9,10},{10,1... | collective-permute-start | bytes 1572872 | tf_op jit(solution)/shard_map/while/body/eval_jaxpr/ppermute | solution.py:16
  53.7 19.4 %collective-permute-start.2 = (bf16[2,256,256]{1,2,0:T(8,128)(2,1)}, bf16[2,256,256]{1,2,0:T(8,128)(2,1)}, u32[]{:S(2)}, u32[]{:S(2)}) collective-permute-start(bf16[2,256,256]{1,2,0:T(8,128)(2,1)} %copy.282), channel_id=1, source_target_pairs={{0,1},{1,2},{2,3},{3,4},{4,5},{5,6},{6,7},{7,8},{8,9},{9,10},{10,1... | collective-permute-start | bytes 786440 | tf_op jit(solution)/shard_map/while/body/eval_jaxpr/ppermute | solution.py:16
  80.0 26.3 %collective-permute-start.3 = (f32[2,256,256]{1,2,0:T(8,128)S(1)}, f32[2,256,256]{1,2,0:T(8,128)S(1)}, u32[]{:S(2)}, u32[]{:S(2)}) collective-permute-start(f32[2,256,256]{1,2,0:T(8,128)S(1)} %add.258), channel_id=1, source_target_pairs={{0,1},{1,2},{2,3},{3,4},{4,5},{5,6},{6,7},{7,8},{8,9},{9,10},{10,1... | collective-permute-start | bytes 1572872 | tf_op jit(solution)/shard_map/while/body/eval_jaxpr/ppermute | solution.py:16
  88.8 17.5 %collective-permute-start.2 = (bf16[2,256,256]{1,2,0:T(8,128)(2,1)}, bf16[2,256,256]{1,2,0:T(8,128)(2,1)}, u32[]{:S(2)}, u32[]{:S(2)}) collective-permute-start(bf16[2,256,256]{1,2,0:T(8,128)(2,1)} %copy.282), channel_id=1, source_target_pairs={{0,1},{1,2},{2,3},{3,4},{4,5},{5,6},{6,7},{7,8},{8,9},{9,10},{10,1... | collective-permute-start | bytes 786440 | tf_op jit(solution)/shard_map/while/body/eval_jaxpr/ppermute | solution.py:16
  113.2 22.8 %collective-permute-start.3 = (f32[2,256,256]{1,2,0:T(8,128)S(1)}, f32[2,256,256]{1,2,0:T(8,128)S(1)}, u32[]{:S(2)}, u32[]{:S(2)}) collective-permute-start(f32[2,256,256]{1,2,0:T(8,128)S(1)} %add.258), channel_id=1, source_target_pairs={{0,1},{1,2},{2,3},{3,4},{4,5},{5,6},{6,7},{7,8},{8,9},{9,10},{10,1... | collective-permute-start | bytes 1572872 | tf_op jit(solution)/shard_map/while/body/eval_jaxpr/ppermute | solution.py:16
  113.3 22.7 %collective-permute-start.2 = (bf16[2,256,256]{1,2,0:T(8,128)(2,1)}, bf16[2,256,256]{1,2,0:T(8,128)(2,1)}, u32[]{:S(2)}, u32[]{:S(2)}) collective-permute-start(bf16[2,256,256]{1,2,0:T(8,128)(2,1)} %copy.282), channel_id=1, source_target_pairs={{0,1},{1,2},{2,3},{3,4},{4,5},{5,6},{6,7},{7,8},{8,9},{9,10},{10,1... | collective-permute-start | bytes 786440 | tf_op jit(solution)/shard_map/while/body/eval_jaxpr/ppermute | solution.py:16
  142.9 20.4 %collective-permute-start.3 = (f32[2,256,256]{1,2,0:T(8,128)S(1)}, f32[2,256,256]{1,2,0:T(8,128)S(1)}, u32[]{:S(2)}, u32[]{:S(2)}) collective-permute-start(f32[2,256,256]{1,2,0:T(8,128)S(1)} %add.258), channel_id=1, source_target_pairs={{0,1},{1,2},{2,3},{3,4},{4,5},{5,6},{6,7},{7,8},{8,9},{9,10},{10,1... | collective-permute-start | bytes 1572872 | tf_op jit(solution)/shard_map/while/body/eval_jaxpr/ppermute | solution.py:16
  144.4 18.9 %collective-permute-start.2 = (bf16[2,256,256]{1,2,0:T(8,128)(2,1)}, bf16[2,256,256]{1,2,0:T(8,128)(2,1)}, u32[]{:S(2)}, u32[]{:S(2)}) collective-permute-start(bf16[2,256,256]{1,2,0:T(8,128)(2,1)} %copy.282), channel_id=1, source_target_pairs={{0,1},{1,2},{2,3},{3,4},{4,5},{5,6},{6,7},{7,8},{8,9},{9,10},{10,1... | collective-permute-start | bytes 786440 | tf_op jit(solution)/shard_map/while/body/eval_jaxpr/ppermute | solution.py:16
  179.3 19.2 %collective-permute-start.3 = (f32[2,256,256]{1,2,0:T(8,128)S(1)}, f32[2,256,256]{1,2,0:T(8,128)S(1)}, u32[]{:S(2)}, u32[]{:S(2)}) collective-permute-start(f32[2,256,256]{1,2,0:T(8,128)S(1)} %add.258), channel_id=1, source_target_pairs={{0,1},{1,2},{2,3},{3,4},{4,5},{5,6},{6,7},{7,8},{8,9},{9,10},{10,1... | collective-permute-start | bytes 1572872 | tf_op jit(solution)/shard_map/while/body/eval_jaxpr/ppermute | solution.py:16
  181.7 16.9 %collective-permute-start.2 = (bf16[2,256,256]{1,2,0:T(8,128)(2,1)}, bf16[2,256,256]{1,2,0:T(8,128)(2,1)}, u32[]{:S(2)}, u32[]{:S(2)}) collective-permute-start(bf16[2,256,256]{1,2,0:T(8,128)(2,1)} %copy.282), channel_id=1, source_target_pairs={{0,1},{1,2},{2,3},{3,4},{4,5},{5,6},{6,7},{7,8},{8,9},{9,10},{10,1... | collective-permute-start | bytes 786440 | tf_op jit(solution)/shard_map/while/body/eval_jaxpr/ppermute | solution.py:16
  205.5 23.3 %collective-permute-start.3 = (f32[2,256,256]{1,2,0:T(8,128)S(1)}, f32[2,256,256]{1,2,0:T(8,128)S(1)}, u32[]{:S(2)}, u32[]{:S(2)}) collective-permute-start(f32[2,256,256]{1,2,0:T(8,128)S(1)} %add.258), channel_id=1, source_target_pairs={{0,1},{1,2},{2,3},{3,4},{4,5},{5,6},{6,7},{7,8},{8,9},{9,10},{10,1... | collective-permute-start | bytes 1572872 | tf_op jit(solution)/shard_map/while/body/eval_jaxpr/ppermute | solution.py:16
  213.5 15.3 %collective-permute-start.2 = (bf16[2,256,256]{1,2,0:T(8,128)(2,1)}, bf16[2,256,256]{1,2,0:T(8,128)(2,1)}, u32[]{:S(2)}, u32[]{:S(2)}) collective-permute-start(bf16[2,256,256]{1,2,0:T(8,128)(2,1)} %copy.282), channel_id=1, source_target_pairs={{0,1},{1,2},{2,3},{3,4},{4,5},{5,6},{6,7},{7,8},{8,9},{9,10},{10,1... | collective-permute-start | bytes 786440 | tf_op jit(solution)/shard_map/while/body/eval_jaxpr/ppermute | solution.py:16
  235.8 30.6 %collective-permute-start.3 = (f32[2,256,256]{1,2,0:T(8,128)S(1)}, f32[2,256,256]{1,2,0:T(8,128)S(1)}, u32[]{:S(2)}, u32[]{:S(2)}) collective-permute-start(f32[2,256,256]{1,2,0:T(8,128)S(1)} %add.258), channel_id=1, source_target_pairs={{0,1},{1,2},{2,3},{3,4},{4,5},{5,6},{6,7},{7,8},{8,9},{9,10},{10,1... | collective-permute-start | bytes 1572872 | tf_op jit(solution)/shard_map/while/body/eval_jaxpr/ppermute | solution.py:16
  282.4 22.2 %collective-permute-start.3 = (f32[2,256,256]{1,2,0:T(8,128)S(1)}, f32[2,256,256]{1,2,0:T(8,128)S(1)}, u32[]{:S(2)}, u32[]{:S(2)}) collective-permute-start(f32[2,256,256]{1,2,0:T(8,128)S(1)} %add.258), channel_id=1, source_target_pairs={{0,1},{1,2},{2,3},{3,4},{4,5},{5,6},{6,7},{7,8},{8,9},{9,10},{10,1... | collective-permute-start | bytes 1572872 | tf_op jit(solution)/shard_map/while/body/eval_jaxpr/ppermute | solution.py:16
  320.5 17.1 %collective-permute-start.3 = (f32[2,256,256]{1,2,0:T(8,128)S(1)}, f32[2,256,256]{1,2,0:T(8,128)S(1)}, u32[]{:S(2)}, u32[]{:S(2)}) collective-permute-start(f32[2,256,256]{1,2,0:T(8,128)S(1)} %add.258), channel_id=1, source_target_pairs={{0,1},{1,2},{2,3},{3,4},{4,5},{5,6},{6,7},{7,8},{8,9},{9,10},{10,1... | collective-permute-start | bytes 1572872 | tf_op jit(solution)/shard_map/while/body/eval_jaxpr/ppermute | solution.py:16
  320.6 17.0 %collective-permute-start.2 = (bf16[2,256,256]{1,2,0:T(8,128)(2,1)}, bf16[2,256,256]{1,2,0:T(8,128)(2,1)}, u32[]{:S(2)}, u32[]{:S(2)}) collective-permute-start(bf16[2,256,256]{1,2,0:T(8,128)(2,1)} %copy.282), channel_id=1, source_target_pairs={{0,1},{1,2},{2,3},{3,4},{4,5},{5,6},{6,7},{7,8},{8,9},{9,10},{10,1... | collective-permute-start | bytes 786440 | tf_op jit(solution)/shard_map/while/body/eval_jaxpr/ppermute | solution.py:16
  353.6 20.5 %collective-permute-start.3 = (f32[2,256,256]{1,2,0:T(8,128)S(1)}, f32[2,256,256]{1,2,0:T(8,128)S(1)}, u32[]{:S(2)}, u32[]{:S(2)}) collective-permute-start(f32[2,256,256]{1,2,0:T(8,128)S(1)} %add.258), channel_id=1, source_target_pairs={{0,1},{1,2},{2,3},{3,4},{4,5},{5,6},{6,7},{7,8},{8,9},{9,10},{10,1... | collective-permute-start | bytes 1572872 | tf_op jit(solution)/shard_map/while/body/eval_jaxpr/ppermute | solution.py:16
  356.2 17.9 %collective-permute-start.2 = (bf16[2,256,256]{1,2,0:T(8,128)(2,1)}, bf16[2,256,256]{1,2,0:T(8,128)(2,1)}, u32[]{:S(2)}, u32[]{:S(2)}) collective-permute-start(bf16[2,256,256]{1,2,0:T(8,128)(2,1)} %copy.282), channel_id=1, source_target_pairs={{0,1},{1,2},{2,3},{3,4},{4,5},{5,6},{6,7},{7,8},{8,9},{9,10},{10,1... | collective-permute-start | bytes 786440 | tf_op jit(solution)/shard_map/while/body/eval_jaxpr/ppermute | solution.py:16
  381.0 28.7 %collective-permute-start.3 = (f32[2,256,256]{1,2,0:T(8,128)S(1)}, f32[2,256,256]{1,2,0:T(8,128)S(1)}, u32[]{:S(2)}, u32[]{:S(2)}) collective-permute-start(f32[2,256,256]{1,2,0:T(8,128)S(1)} %add.258), channel_id=1, source_target_pairs={{0,1},{1,2},{2,3},{3,4},{4,5},{5,6},{6,7},{7,8},{8,9},{9,10},{10,1... | collective-permute-start | bytes 1572872 | tf_op jit(solution)/shard_map/while/body/eval_jaxpr/ppermute | solution.py:16
  392.6 17.1 %collective-permute-start.2 = (bf16[2,256,256]{1,2,0:T(8,128)(2,1)}, bf16[2,256,256]{1,2,0:T(8,128)(2,1)}, u32[]{:S(2)}, u32[]{:S(2)}) collective-permute-start(bf16[2,256,256]{1,2,0:T(8,128)(2,1)} %copy.282), channel_id=1, source_target_pairs={{0,1},{1,2},{2,3},{3,4},{4,5},{5,6},{6,7},{7,8},{8,9},{9,10},{10,1... | collective-permute-start | bytes 786440 | tf_op jit(solution)/shard_map/while/body/eval_jaxpr/ppermute | solution.py:16
  416.6 21.2 %collective-permute-start.3 = (f32[2,256,256]{1,2,0:T(8,128)S(1)}, f32[2,256,256]{1,2,0:T(8,128)S(1)}, u32[]{:S(2)}, u32[]{:S(2)}) collective-permute-start(f32[2,256,256]{1,2,0:T(8,128)S(1)} %add.258), channel_id=1, source_target_pairs={{0,1},{1,2},{2,3},{3,4},{4,5},{5,6},{6,7},{7,8},{8,9},{9,10},{10,1... | collective-permute-start | bytes 1572872 | tf_op jit(solution)/shard_map/while/body/eval_jaxpr/ppermute | solution.py:16
  453.9 16.7 %collective-permute-start.3 = (f32[2,256,256]{1,2,0:T(8,128)S(1)}, f32[2,256,256]{1,2,0:T(8,128)S(1)}, u32[]{:S(2)}, u32[]{:S(2)}) collective-permute-start(f32[2,256,256]{1,2,0:T(8,128)S(1)} %add.258), channel_id=1, source_target_pairs={{0,1},{1,2},{2,3},{3,4},{4,5},{5,6},{6,7},{7,8},{8,9},{9,10},{10,1... | collective-permute-start | bytes 1572872 | tf_op jit(solution)/shard_map/while/body/eval_jaxpr/ppermute | solution.py:16
  477.5 25.1 %collective-permute-start.3 = (f32[2,256,256]{1,2,0:T(8,128)S(1)}, f32[2,256,256]{1,2,0:T(8,128)S(1)}, u32[]{:S(2)}, u32[]{:S(2)}) collective-permute-start(f32[2,256,256]{1,2,0:T(8,128)S(1)} %add.258), channel_id=1, source_target_pairs={{0,1},{1,2},{2,3},{3,4},{4,5},{5,6},{6,7},{7,8},{8,9},{9,10},{10,1... | collective-permute-start | bytes 1572872 | tf_op jit(solution)/shard_map/while/body/eval_jaxpr/ppermute | solution.py:16
  509.2 500.5 %collective-permute-start.5 = (f32[2,256,256]{2,1,0:T(8,128)}, f32[2,256,256]{2,1,0:T(8,128)}, u32[]{:S(2)}, u32[]{:S(2)}) collective-permute-start(f32[2,256,256]{2,1,0:T(8,128)} %add.207), channel_id=1, source_target_pairs={{0,1},{1,2},{2,3},{3,4},{4,5},{5,6},{6,7},{7,8},{8,9},{9,10},{10,1... | collective-permute-start | bytes 1572872 | tf_op jit(solution)/shard_map/ppermute | solution.py:16
  541.6 17.5 %collective-permute-start.1 = (f32[2,256,256]{1,2,0:T(8,128)S(1)}, f32[2,256,256]{1,2,0:T(8,128)S(1)}, u32[]{:S(2)}, u32[]{:S(2)}) collective-permute-start(f32[2,256,256]{1,2,0:T(8,128)S(1)} %add.252), channel_id=1, source_target_pairs={{0,16},{16,32},{32,48},{48,64},{64,80},{80,96},{96,112},{112,128},... | collective-permute-start | bytes 1572872 | tf_op jit(solution)/shard_map/while/body/eval_jaxpr/ppermute | solution.py:16
  575.1 15.2 %collective-permute-start.1 = (f32[2,256,256]{1,2,0:T(8,128)S(1)}, f32[2,256,256]{1,2,0:T(8,128)S(1)}, u32[]{:S(2)}, u32[]{:S(2)}) collective-permute-start(f32[2,256,256]{1,2,0:T(8,128)S(1)} %add.252), channel_id=1, source_target_pairs={{0,16},{16,32},{32,48},{48,64},{64,80},{80,96},{96,112},{112,128},... | collective-permute-start | bytes 1572872 | tf_op jit(solution)/shard_map/while/body/eval_jaxpr/ppermute | solution.py:16
  606.3 15.2 %collective-permute-start.1 = (f32[2,256,256]{1,2,0:T(8,128)S(1)}, f32[2,256,256]{1,2,0:T(8,128)S(1)}, u32[]{:S(2)}, u32[]{:S(2)}) collective-permute-start(f32[2,256,256]{1,2,0:T(8,128)S(1)} %add.252), channel_id=1, source_target_pairs={{0,16},{16,32},{32,48},{48,64},{64,80},{80,96},{96,112},{112,128},... | collective-permute-start | bytes 1572872 | tf_op jit(solution)/shard_map/while/body/eval_jaxpr/ppermute | solution.py:16
  637.5 15.2 %collective-permute-start.1 = (f32[2,256,256]{1,2,0:T(8,128)S(1)}, f32[2,256,256]{1,2,0:T(8,128)S(1)}, u32[]{:S(2)}, u32[]{:S(2)}) collective-permute-start(f32[2,256,256]{1,2,0:T(8,128)S(1)} %add.252), channel_id=1, source_target_pairs={{0,16},{16,32},{32,48},{48,64},{64,80},{80,96},{96,112},{112,128},... | collective-permute-start | bytes 1572872 | tf_op jit(solution)/shard_map/while/body/eval_jaxpr/ppermute | solution.py:16
  846.9 18.2 %collective-permute-start.1 = (f32[2,256,256]{1,2,0:T(8,128)S(1)}, f32[2,256,256]{1,2,0:T(8,128)S(1)}, u32[]{:S(2)}, u32[]{:S(2)}) collective-permute-start(f32[2,256,256]{1,2,0:T(8,128)S(1)} %add.252), channel_id=1, source_target_pairs={{0,16},{16,32},{32,48},{48,64},{64,80},{80,96},{96,112},{112,128},... | collective-permute-start | bytes 1572872 | tf_op jit(solution)/shard_map/while/body/eval_jaxpr/ppermute | solution.py:16
  847.0 18.1 %collective-permute-start = (bf16[2,256,256]{1,2,0:T(8,128)(2,1)}, bf16[2,256,256]{1,2,0:T(8,128)(2,1)}, u32[]{:S(2)}, u32[]{:S(2)}) collective-permute-start(bf16[2,256,256]{1,2,0:T(8,128)(2,1)} %copy.298), channel_id=1, source_target_pairs={{0,16},{16,32},{32,48},{48,64},{64,80},{80,96},{96,112},{112,128},... | collective-permute-start | bytes 786440 | tf_op jit(solution)/shard_map/while/body/eval_jaxpr/ppermute | solution.py:16
  (133 other events, 1837.6 us)
where the time goes:
time: 1030 us; the launch traced here: 1020 us
  waiting for transfers between devices  361 us (35%)
  local copies, waits for them, and re-layouts  208 us (20%)
  starting transfers between devices  186 us (18%)
  other arithmetic  166 us (16%)
  matrix products  77.7 us (8%)
  loops' own time  21.7 us (2%)
    ppermute x62, waiting for transfers between devices, shifted(): return lax.ppermute(value, axis, pairs)  361 us
    ppermute x62, starting transfers between devices, shifted(): return lax.ppermute(value, axis, pairs)  186 us
    while x210, local copies, waits for them, and re-layouts  74.3 us
    add x30, other arithmetic, advance(): grad_q + add_q  53 us
    reshape x40, local copies, waits for them, and re-layouts, key_side_terms(): jnp.stack([grad_k.reshape(holding * BLOCK, width), grad_v.reshape(holding...  41.5 us
    add x30, other arithmetic, advance(): partial_value + add_part  38.8 us
    another operation x20, other arithmetic, key_side_terms(): jnp.stack([grad_k.reshape(holding * BLOCK, width), grad_v.reshape(holding...  34.8 us
    dot_general x20, matrix products, attention_parts(): jnp.einsum('bqhd,ckhd->bchqk', grad_blocks, near_values, preferred_elemen...  27.7 us
  transfers between devices with their start and end apart: 62, of which 31 were waited for; matrix products, arithmetic and copies ran while one was open for 27% of the time, Pallas kernels for 0%

commit v1 on v0

v1 whole, which is shorter than its diff:
```python
import math

import jax
import jax.numpy as jnp
from jax import lax
from jax.experimental import pallas as pl
from jax.experimental.pallas import tpu as pltpu
from jax.sharding import PartitionSpec as P

HEADS = 8
HEAD_DIM = 32
BLOCK = 128
ROWS = 256
D = 256
N_Z, N_Y = 8, 4
Q_SLOTS = 11
K_SLOTS = 5
META = 24
HIDE = 1e30
SCALING = 1.0 / math.sqrt(HEAD_DIM)
LOG2E = math.log2(math.e)
MESH = pl.DeviceIdType.MESH
ANY = pl.BlockSpec(memory_space=pl.ANY)
VMEM = pl.BlockSpec(memory_space=pltpu.VMEM)
SMEM = pl.BlockSpec(memory_space=pltpu.SMEM)
VMEM_LIMIT = 56 * 1024 * 1024
FAR, NEAR, ACROSS = 0, 1, 2
STEPS = (
    (0, NEAR), (0, FAR), (1, FAR), (7, FAR), (8, NEAR), (0, ACROSS), (8, ACROSS), (2, FAR),
    (6, FAR), (4, FAR), (3, FAR), (5, FAR), (10, ACROSS), (9, ACROSS), (10, NEAR), (9, NEAR),
)
KEY_SLOTS = {FAR: (0, 1), NEAR: (0, 2), ACROSS: (3, 4)}
NT = (((1,), (1,)), ((), ()))
NN = (((1,), (0,)), ((), ()))


def dot(a, b, dims):
    return lax.dot_general(a, b, dims, preferred_element_type=jnp.float32)


def places():
    g, m = lax.axis_index("grp"), lax.axis_index("dom")
    return g // 4, g // 2 % 2, g % 2, m // 2, m % 2


def partners(y, xh, c, z, xl):
    def at(y=y, xh=xh, c=c, z=z, xl=xl):
        return ((y * 2 + xh) * 2 + c, z * 2 + xl)

    return {
        "right": at(z=(z + 1) % N_Z),
        "left": at(z=(z + N_Z - 1) % N_Z),
        "y1": at(y=(y + 1) % N_Y),
        "y2": at(y=(y + 2) % N_Y),
        "y3": at(y=(y + 3) % N_Y),
        "far_x": at(xh=1 - xh),
        "near_x": at(xl=1 - xl),
        "sibling": at(c=1 - c),
    }


def meet(others):
    barrier = pltpu.get_barrier_semaphore()
    for device in others.values():
        pl.semaphore_signal(barrier, inc=1, device_id=device, device_id_type=MESH)
    pl.semaphore_wait(barrier, len(others))


def kernel(
    q_ref, g_ref, o_ref, k_ref, v_ref, lse_ref, ll_ref, el_ref, lc_ref, ec_ref,
    qg_ref, kg_ref, vg_ref,
    qb, gb, ob, qt, gt, meta, kk, vv, km, vm, kt, dqa, dka, dva,
    ring_out, ring_in, y_out, y_in, x_out, x_in,
    in_sem, ring_send, ring_recv, y_send, y_recv, x_send, x_recv,
    rr_send, rr_recv, ry_send, ry_recv, rx_send, rx_recv,
):
    y, xh, c, z, xl = places()
    others = partners(y, xh, c, z, xl)
    f32, bf16 = jnp.float32, jnp.bfloat16

    def remote(src, dst, send, recv, who):
        return pltpu.make_async_remote_copy(
            src_ref=src, dst_ref=dst, send_sem=send, recv_sem=recv,
            device_id=others[who], device_id_type=MESH,
        )

    held = (qt, gt, meta)
    halves = ((0, BLOCK), (0, BLOCK), (0, 16))
    sizes = ((BLOCK, BLOCK), (BLOCK, BLOCK), (16, 8))

    def ring(hop, kind, way):
        whole = held[kind]
        src, dst = ((N_Z - hop) % N_Z, N_Z - 1 - hop) if way == 0 else (hop, hop + 1)
        src, dst = whole.at[src], whole.at[dst]
        if hop == 3:
            start = 0 if way == 0 else sizes[kind][0]
            rows = pl.ds(start, sizes[kind][way])
            src, dst = src.at[rows], dst.at[rows]
        return remote(
            src, dst, ring_send.at[hop, kind, way], ring_recv.at[hop, kind, way],
            "right" if way == 0 else "left",
        )

    def ycopy(step, kind):
        whole = held[kind]
        return remote(
            whole.at[0], whole.at[N_Z - 1 + N_Y - step], y_send.at[step - 1, kind],
            y_recv.at[step - 1, kind], f"y{step}",
        )

    def xcopy(what, i):
        whole, own = (kk, k_ref) if i == 0 else (vv, v_ref)
        number, who = {"near": (0, "near_x"), "sib": (1, "sibling"), "far": (2, "far_x"), "on": (3, "sibling")}[what]
        src = whole.at[3] if what == "on" else own
        return remote(src, whole.at[number + 1], x_send.at[number, i], x_recv.at[number, i], who)

    def ring_back(hop, way):
        buf, into = ring_out.at[hop, way], ring_in.at[hop, way]
        if hop == 0:
            rows = pl.ds(0 if way == 0 else BLOCK, BLOCK)
            buf, into = buf.at[rows], into.at[rows]
        return remote(buf, into, rr_send.at[hop, way], rr_recv.at[hop, way], "right" if way == 0 else "left")

    def y_back(step):
        return remote(y_out.at[step - 1], y_in.at[step - 1], ry_send.at[step - 1], ry_recv.at[step - 1], f"y{step}")

    def x_back(what, i):
        number, who = {"near": (0, "near_x"), "sib": (1, "sibling"), "pass": (2, "sibling"), "far": (3, "far_x")}[what]
        return remote(x_out.at[number, i], x_in.at[number, i], rx_send.at[number, i], rx_recv.at[number, i], who)

    loads = [
        pltpu.make_async_copy(src, dst, in_sem.at[i])
        for i, (src, dst) in enumerate(
            ((q_ref, qb), (g_ref, gb), (o_ref, ob), (k_ref, kk.at[0]), (v_ref, vv.at[0]))
        )
    ]
    for load in loads:
        load.start()

    lane = lax.broadcasted_iota(jnp.int32, (8, 128), 1)

    def mark(lists, counts, e, base):
        def one(s, hidden):
            hit = (lane == base + lists[e, s]) & (s < counts[e])
            return jnp.where(hit, 0.0, hidden)
        return one

    hidden = jnp.full((8, 128), HIDE, f32)
    for e in range(2):
        hidden = lax.fori_loop(0, ll_ref.shape[1], mark(ll_ref, lc_ref, e, e * 64), hidden)
        hidden = lax.fori_loop(0, el_ref.shape[1], mark(el_ref, ec_ref, e, e * 64 + 32), hidden)
    meta[0, 16:24, 0:128] = hidden
    meta[0, 16:24, 128:256] = hidden
    meta[0, 0:HEADS, :] = lse_ref[...] * LOG2E

    meet(others)
    for i in range(2):
        for what in ("near", "sib", "far"):
            xcopy(what, i).start()
    loads[0].wait()
    qt[0] = qb[...].astype(f32).T.astype(bf16)
    for way in range(2):
        ring(0, 0, way).start()
    for step in (1, 3):
        ycopy(step, 0).start()
    loads[1].wait()
    gt[0] = gb[...].astype(f32).T.astype(bf16)
    for way in range(2):
        ring(0, 1, way).start()
    for step in (1, 3):
        ycopy(step, 1).start()
    loads[2].wait()
    product = gb[...].astype(f32) * ob[...].astype(f32)
    high = product.astype(bf16)
    low = (product - high.astype(f32)).astype(bf16)
    rows_of = lax.broadcasted_iota(jnp.int32, (HEADS, D), 0)
    cols_of = lax.broadcasted_iota(jnp.int32, (HEADS, D), 1)
    pick = jnp.where(cols_of // HEAD_DIM == rows_of, 1.0, 0.0).astype(bf16)
    meta[0, HEADS:2 * HEADS, :] = dot(pick, high, NT) + dot(pick, low, NT)
    for way in range(2):
        ring(0, 2, way).start()
    for step in (1, 3):
        ycopy(step, 2).start()
    for kind in range(3):
        ycopy(2, kind).start()

    dqa[...] = jnp.zeros_like(dqa)
    dka[...] = jnp.zeros_like(dka)
    dva[...] = jnp.zeros_like(dva)
    head_of = lax.broadcasted_iota(jnp.int32, (1, 128), 1) // HEAD_DIM
    masks = [jnp.where(head_of == h, 1.0, 0.0).astype(bf16) for h in range(4)]

    def spread(slot):
        kt[slot] = kk[slot].astype(f32).T.astype(bf16)
        for h in range(HEADS):
            cols = slice(h // 4 * 128, h // 4 * 128 + 128)
            km[slot, h] = kk[slot, :, cols] * masks[h % 4]
            vm[slot, h] = vv[slot, :, cols] * masks[h % 4]

    def arrive(what):
        for i in range(2):
            xcopy(what, i).wait_recv()

    def pass_on(hop):
        for kind in range(3):
            for way in range(2):
                ring(hop - 1, kind, way).wait_recv()
                ring(hop, kind, way).start()

    def y_arrive(step):
        for kind in range(3):
            ycopy(step, kind).wait_recv()

    def send_back(hop):
        for way in range(2):
            slot = 4 - hop if way == 0 else 4 + hop
            if hop == 0:
                rows = slice(0, BLOCK) if way == 0 else slice(BLOCK, ROWS)
                ring_out[0, way, rows] = (dqa[slot, rows] * SCALING).astype(bf16)
            else:
                ring_back(hop - 1, way).wait_recv()
                if hop == 1:
                    rows, rest = slice(0, BLOCK), slice(BLOCK, ROWS)
                    if way == 1:
                        rows, rest = rest, rows
                    ring_out[1, way, rows] = (
                        dqa[slot, rows] * SCALING + ring_in[0, way, rows].astype(f32)
                    ).astype(bf16)
                    ring_out[1, way, rest] = (dqa[slot, rest] * SCALING).astype(bf16)
                else:
                    ring_out[hop, way] = (
                        dqa[slot] * SCALING + ring_in[hop - 1, way].astype(f32)
                    ).astype(bf16)
            ring_back(hop, way).start()

    def y_send_back(step):
        y_out[step - 1] = (dqa[N_Z - 1 + step] * SCALING).astype(bf16)
        y_back(step).start()

    def x_send_back(what, number, slot):
        x_out[number, 0] = (dka[slot] * SCALING).astype(bf16)
        x_back(what, 0).start()
        x_out[number, 1] = dva[slot].astype(bf16)
        x_back(what, 1).start()

    def far_send_back():
        x_back("pass", 0).wait_recv()
        x_out[3, 0] = (dka[3] * SCALING + x_in[2, 0].astype(f32)).astype(bf16)
        x_back("far", 0).start()
        x_back("pass", 1).wait_recv()
        x_out[3, 1] = (dva[3] + x_in[2, 1].astype(f32)).astype(bf16)
        x_back("far", 1).start()

    def at_1():
        pass_on(1)
        arrive("near")
        spread(1)

    def at_3():
        arrive("far")
        for i in range(2):
            xcopy("on", i).start()
        spread(3)

    def at_4():
        pass_on(2)
        y_arrive(3)

    def at_5():
        arrive("on")
        spread(4)

    def at_7():
        pass_on(3)

    def at_9():
        for kind in range(3):
            for way in range(2):
                ring(3, kind, way).wait_recv()

    def at_10():
        send_back(0)
        y_send_back(1)

    def at_12():
        send_back(1)
        x_send_back("near", 0, 1)
        y_arrive(1)
        y_arrive(2)

    def at_14():
        send_back(2)
        x_send_back("pass", 2, 4)

    def at_15():
        far_send_back()
        y_send_back(3)

    events = {1: at_1, 3: at_3, 4: at_4, 5: at_5, 7: at_7, 9: at_9, 10: at_10, 12: at_12, 14: at_14, 15: at_15}

    spread_loads = loads[3:]
    for load in spread_loads:
        load.wait()
    spread(0)
    arrive("sib")
    spread(2)

    def table(s, values):
        found = jnp.int32(values[0])
        for i, value in enumerate(values):
            if i > 0 and value != values[0]:
                found = jnp.where(s == i, jnp.int32(value), found)
        return found

    far_at = 32 + z * 4
    near_at = y * 8 + xh * 4
    across_at = y * 8 + (1 - xh) * 4
    one_lane = lax.broadcasted_iota(jnp.int32, (1, 128), 1)

    def step(s, carry):
        for at, event in events.items():
            pl.when(s == at)(event)
        qd = table(s, [slot for slot, _ in STEPS])
        kind = table(s, [k for _, k in STEPS])
        key_slots = [table(s, [KEY_SLOTS[k][i] for _, k in STEPS]) for i in range(2)]
        start = jnp.where(kind == FAR, far_at, jnp.where(kind == NEAR, near_at, across_at))
        own = jnp.where(kind == FAR, xl, c)
        places_of = [start + own * 2, start + (1 - own) * 2]
        shown = meta[qd, 16:17, 0:128]
        hide = {}
        for i in range(2):
            for ke in range(2):
                cells = [
                    jnp.sum(jnp.where(one_lane == places_of[i] + (e * 64 + ke), shown, 0.0), axis=1, keepdims=True)
                    for e in range(2)
                ]
                hide[i, ke] = jnp.concatenate([jnp.broadcast_to(cell, (1, 128)) for cell in cells], axis=1)
        tiles = [(i, h) for i in range(2) for h in range(HEADS)]

        def first(tile):
            i, h = tile
            cols = slice(h // 4 * 128, h // 4 * 128 + 128)
            return (
                dot(km[key_slots[i], h], qt[qd, cols, :], NN),
                dot(vm[key_slots[i], h], gt[qd, cols, :], NN),
            )

        def second(tile, scores, grad_p):
            i, h = tile
            lse, delta = meta[qd, h:h + 1, :], meta[qd, HEADS + h:HEADS + h + 1, :]
            low, grads = [], []
            for ke in range(2):
                rows = slice(ke * BLOCK, ke * BLOCK + BLOCK)
                attention = jnp.exp2(scores[rows] * (SCALING * LOG2E) - (lse + hide[i, ke]))
                low.append(attention.astype(bf16))
                grads.append((attention * (grad_p[rows] - delta)).astype(bf16))
            return jnp.concatenate(low, axis=0), jnp.concatenate(grads, axis=0)

        def third(tile, low, grads):
            i, h = tile
            rows = slice(h * HEAD_DIM, h * HEAD_DIM + HEAD_DIM)
            dva[key_slots[i], rows] += dot(gt[qd, rows, :], low, NT)
            dka[key_slots[i], rows] += dot(qt[qd, rows, :], grads, NT)
            dqa[qd, rows] += dot(kt[key_slots[i], rows, :], grads, NN)

        ones, twos = {}, {}
        for n in range(len(tiles) + 2):
            if n < len(tiles):
                ones[n] = first(tiles[n])
            if 0 <= n - 1 < len(tiles):
                twos[n - 1] = second(tiles[n - 1], *ones.pop(n - 1))
            if 0 <= n - 2 < len(tiles):
                third(tiles[n - 2], *twos.pop(n - 2))
        return carry

    lax.fori_loop(0, len(STEPS), step, 0)

    y_send_back(2)
    x_send_back("sib", 1, 2)
    send_back(3)
    for i, (out, own) in enumerate(((kg_ref, dka), (vg_ref, dva))):
        total = own[0] * SCALING if i == 0 else own[0]
        for number, what in ((0, "near"), (1, "sib"), (3, "far")):
            x_back(what, i).wait_recv()
            total = total + x_in[number, i].astype(f32)
        out[...] = total.T.astype(bf16)
    total = dqa[0] * SCALING
    for s in (1, 3, 2):
        y_back(s).wait_recv()
        total = total + y_in[s - 1].astype(f32)
    for way in range(2):
        ring_back(3, way).wait_recv()
        total = total + ring_in[3, way].astype(f32)
    qg_ref[...] = total.T.astype(bf16)

    for hop in range(4):
        for way in range(2):
            for kind in range(3):
                ring(hop, kind, way).wait_send()
            ring_back(hop, way).wait_send()
    for s in (1, 2, 3):
        for kind in range(3):
            ycopy(s, kind).wait_send()
        y_back(s).wait_send()
    for i in range(2):
        for what in ("near", "sib", "far", "on"):
            xcopy(what, i).wait_send()
        for what in ("near", "sib", "pass", "far"):
            x_back(what, i).wait_send()


def body(
    queries, key_rows, value_rows, saved_output, output_grad, log_norm,
    local_lists, expander_lists, local_counts, expander_counts,
):
    bf16, f32 = jnp.bfloat16, jnp.float32
    dma = pltpu.SemaphoreType.DMA
    tile = (ROWS, D)
    return tuple(pl.pallas_call(
        kernel,
        name="backward",
        out_shape=[jax.ShapeDtypeStruct(tile, bf16)] * 3,
        in_specs=[ANY] * 5 + [VMEM] + [SMEM] * 4,
        out_specs=[VMEM] * 3,
        scratch_shapes=[
            pltpu.VMEM(tile, bf16), pltpu.VMEM(tile, bf16), pltpu.VMEM(tile, bf16),
            pltpu.VMEM((Q_SLOTS, *tile), bf16), pltpu.VMEM((Q_SLOTS, *tile), bf16),
            pltpu.VMEM((Q_SLOTS, META, ROWS), f32),
            pltpu.VMEM((K_SLOTS, *tile), bf16), pltpu.VMEM((K_SLOTS, *tile), bf16),
            pltpu.VMEM((K_SLOTS, HEADS, ROWS, 128), bf16), pltpu.VMEM((K_SLOTS, HEADS, ROWS, 128), bf16),
            pltpu.VMEM((K_SLOTS, *tile), bf16),
            pltpu.VMEM((Q_SLOTS, *tile), f32),
            pltpu.VMEM((K_SLOTS, *tile), f32), pltpu.VMEM((K_SLOTS, *tile), f32),
            pltpu.VMEM((4, 2, *tile), bf16), pltpu.VMEM((4, 2, *tile), bf16),
            pltpu.VMEM((3, *tile), bf16), pltpu.VMEM((3, *tile), bf16),
            pltpu.VMEM((4, 2, *tile), bf16), pltpu.VMEM((4, 2, *tile), bf16),
            dma((5,)),
            dma((4, 3, 2)), dma((4, 3, 2)), dma((3, 3)), dma((3, 3)), dma((4, 2)), dma((4, 2)),
            dma((4, 2)), dma((4, 2)), dma((3,)), dma((3,)), dma((4, 2)), dma((4, 2)),
        ],
        compiler_params=pltpu.CompilerParams(
            collective_id=0, has_side_effects=True, vmem_limit_bytes=VMEM_LIMIT
        ),
    )(
        queries, output_grad, saved_output, key_rows, value_rows, log_norm,
        local_lists, expander_lists, local_counts, expander_counts,
    ))


def solution(mesh):
    rows = P(("grp", "dom"), None)
    flat = P(("grp", "dom"))
    return jax.shard_map(
        body,
        mesh=mesh,
        in_specs=(rows, rows, rows, rows, rows, P(None, ("grp", "dom")), rows, rows, flat, flat),
        out_specs=(rows, rows, rows),
        check_vma=False,
    )
```

time: 1030 us -> 67.6 us (0.07)
  the two profiles are of different devices: /device:TPU:160 before, /device:TPU:4 now
where the time goes in v1:
time: 67.6 us; the launch traced here: 66.6 us
  Pallas kernels  62.7 us (93%)
  local copies, waits for them, and re-layouts  3.21 us (5%)
    pallas_call x1, Pallas kernels, body(): pl.pallas_call(kernel, name='backward', out_shape=[jax.ShapeDtypeStruct(t...  62.7 us
    unnamed x7, local copies, waits for them, and re-layouts  3.21 us

profile of v1, /device:TPU:4, one launch (start us, length us, event | category | flops | bytes accessed | tf_op | source)
XLA Modules:
  0.0 66.6 jit_solution(11571615820038618697)
XLA Ops:
  0.6 62.7 %backward.1 = (bf16[256,256]{1,0:T(8,128)(2,1)}, bf16[256,256]{1,0:T(8,128)(2,1)}, bf16[256,256]{1,0:T(8,128)(2,1)}) custom-call(bf16[256,256]{1,0:T(8,128)(2,1)} %q_ref.1, bf16[256,256]{1,0:T(8,128)(2,1)} %g_ref.1, bf16[256,256]{1,0:T(8,128)(2,1)} %o_ref.1, bf16[256,256]{1,0:T(8,128)(2,1)} %k_ref.1, bf16[256,256]{1,0:T(8,128)(2,1)} %v_ref.1, ...), custom_call_target="tpu_custom_call" | custom-call | tf_op jit(solution)/shard_map/backward/pallas_call | solution.py:419
  63.3 0.0 copy-start.1
  63.3 1.6 %copy.16 = bf16[256,256]{1,0:T(8,128)(2,1)} copy(bf16[256,256]{1,0:T(8,128)(2,1)} %get-tuple-element.6) | data formatting | bytes 262144
  64.9 0.0 copy-done.1
  65.0 0.0 copy-start
  65.0 0.7 copy.17
  65.6 0.3 copy-done
  65.9 0.7 copy.18
Async XLA Ops:
  63.3 1.6 %copy-start.1 = (bf16[256,256]{1,0:T(8,128)(2,1)S(1)}, bf16[256,256]{1,0:T(8,128)(2,1)}, u32[]{:S(2)}) copy-start(bf16[256,256]{1,0:T(8,128)(2,1)} %get-tuple-element.7) | copy-start | bytes 393220
  65.0 1.0 %copy-start = (bf16[256,256]{1,0:T(8,128)(2,1)S(1)}, bf16[256,256]{1,0:T(8,128)(2,1)}, u32[]{:S(2)}) copy-start(bf16[256,256]{1,0:T(8,128)(2,1)} %get-tuple-element.8) | copy-start | bytes 393220
